TPU v7x, 128 devices: a whole 4x4x4 slice. The times are simulated.
128 devices in a mesh: blk: 16 (over x, y_hi, core), tile: 8 (over z, y_lo).
Axes of the slice: x: 4, y: 4 (y_hi: 2, y_lo: 2; y = y_hi * 2 + y_lo), z: 4, core: 2. Of those that a mesh axis runs over, the one named last changes fastest.
Arguments:
- residual_traces: bfloat16 [131072, 2048], P(('blk', 'tile')), may hold values from -6 to 6
- time_weights: bfloat16 [1024, 2048, 128], P(('blk', 'tile')), may hold values from -0.125 to 0.125
- lateral_amplitude: bfloat16 [1024, 128, 1024], P(('blk', 'tile')), may hold values from -0.1875 to 0.1875
- intersection_tile: int32 [1024, 1], P(('blk', 'tile')), may hold values from 0 to 7; in each aligned block of 8 rows (0 to 7, 8 to 15, ...) at most 2 rows name the same one
- visit_stop: int32 [1024], P(('blk', 'tile')), may hold values from 0 to 3
Outputs:
- image_tiles: float32 [16384, 128], P(('blk', 'tile'))
Inputs may be any that keep to these rules, and one draw needn't show every extreme that they name: `intersection_tile`: of the 8 table blocks of one device, at most 2 name the same tile; in every draw some device has 2 blocks naming one tile.
All inputs are finite; a program needn't handle non-finite values.
Results may differ from a plain program's by a relative error of at most 0.0029.
Values may be sent and summed in bfloat16 or wider, within the bound.
A program may use at most 128 MiB of HBM per device.

v0:
```python
import jax
import jax.numpy as jnp
from jax import lax
from jax.sharding import PartitionSpec as P

MOST = 2
STOPS = 4


def from_behind(array, axis, by):
    count = lax.axis_size(axis)
    return lax.ppermute(array, axis, [(i, (i + by) % count) for i in range(count)])


def body(residual_traces, time_weights, lateral_amplitude, intersection_tile, visit_stop):
    tiles_count = lax.axis_size("tile")
    slots = tiles_count * MOST
    target = intersection_tile[:, 0]
    blocks_here = target.shape[0]
    order_index = jnp.arange(blocks_here, dtype=jnp.int32)
    earlier = (target[None, :] == target[:, None]) & (order_index[None, :] < order_index[:, None])
    slot_rank = jnp.sum(earlier.astype(jnp.int32), axis=1)
    slot_of = target * MOST + slot_rank
    onehot = (slot_of[:, None] == jnp.arange(slots, dtype=jnp.int32)[None, :]).astype(jnp.bfloat16)
    packed_weight = jnp.einsum(
        "bs,bnd->snd", onehot, time_weights, preferred_element_type=jnp.float32
    ).astype(jnp.bfloat16)
    packed_amplitude = jnp.einsum(
        "bs,blt->slt", onehot, lateral_amplitude, preferred_element_type=jnp.float32
    ).astype(jnp.bfloat16)
    stop_code = jnp.sum(
        onehot.astype(jnp.float32) * (visit_stop + 1).astype(jnp.float32)[:, None], axis=0
    ).astype(jnp.bfloat16)
    samples = time_weights.shape[1]
    depth_count = time_weights.shape[2]
    lateral_count = lateral_amplitude.shape[1]
    trace_count = lateral_amplitude.shape[2]
    packed_weight = packed_weight.reshape(tiles_count, MOST, samples, depth_count)
    packed_amplitude = packed_amplitude.reshape(tiles_count, MOST, lateral_count, trace_count)
    stop_code = stop_code.reshape(tiles_count, MOST)
    got_weight, got_amplitude, got_code = (
        lax.all_to_all(packed_weight, "tile", split_axis=0, concat_axis=0, tiled=True),
        lax.all_to_all(packed_amplitude, "tile", split_axis=0, concat_axis=0, tiled=True),
        lax.all_to_all(stop_code, "tile", split_axis=0, concat_axis=0, tiled=True),
    )
    got_weight = got_weight.reshape(slots, samples, depth_count)
    got_amplitude = got_amplitude.reshape(slots, lateral_count, trace_count)
    got_code = got_code.reshape(slots).astype(jnp.int32)
    visits = [residual_traces]
    for hop_index in range(STOPS - 1):
        visits.append(from_behind(visits[-1], "blk", 1))
    stacked = jnp.stack(visits)

    def spray(image_sum, inputs):
        weight, amplitude, code_value = inputs

        def filled(total):
            stop_index = jnp.maximum(code_value - 1, 0)
            trace_block = lax.dynamic_index_in_dim(stacked, stop_index, 0, keepdims=False)
            projected = jnp.dot(trace_block, weight, preferred_element_type=jnp.float32).astype(
                jnp.bfloat16
            )
            return total + jnp.dot(amplitude, projected, preferred_element_type=jnp.float32)

        def empty_slot(total):
            return total

        return (lax.cond(code_value > 0, filled, empty_slot, image_sum), None)

    image_sum = jnp.zeros((lateral_count, depth_count), jnp.float32)
    image_sum, _ = lax.scan(spray, image_sum, (got_weight, got_amplitude, got_code))
    return image_sum


def solution(mesh):
    in_specs = (
        P(("blk", "tile"), None),
        P(("blk", "tile"), None, None),
        P(("blk", "tile"), None, None),
        P(("blk", "tile"), None),
        P(("blk", "tile")),
    )
    out_specs = P(("blk", "tile"), None)
    return jax.shard_map(body, mesh=mesh, in_specs=in_specs, out_specs=out_specs, check_vma=False)
```

profile of v0, /device:TPU:80, one launch (start us, length us, event | category | flops | bytes accessed | tf_op | source)
XLA Modules:
  0.0 401.8 jit_solution(14210277797188004461)
XLA Ops:
  3.1 5.7 %all-to-all-start = ((bf16[8,1,2]{2,1,0:T(2,128)(2,1)}), bf16[8,1,2]{2,1,0:T(2,128)(2,1)S(1)}, u32[]{:S(2)}, u32[]{:S(2)}) async-start(bf16[8,1,2]{2,1,0:T(2,128)(2,1)} %convert_element_type.57), calls=%async_computation | async-start | bytes 8192 | tf_op jit(solution)/shard_map/all_to_all | solution.py:44
  12.0 7.2 %reshape.34 = bf16[8,2,128,1024]{3,1,0,2:T(2,128)(2,1)} reshape(bf16[16,128,1024]{2,0,1:T(8,128)(2,1)} %convolution_convert_fusion.1) | data formatting | bytes 8388608 | tf_op jit(solution)/shard_map/reshape | solution.py:39
  19.1 7.0 %copy.28 = bf16[8,2,128,1024]{3,1,2,0:T(2,128)(2,1)} copy(bf16[8,2,128,1024]{3,1,0,2:T(2,128)(2,1)} %reshape.34) | data formatting | bytes 8388608 | tf_op jit(solution)/shard_map/reshape | solution.py:39
  26.2 5.7 %all-to-all-start.1 = ((bf16[8,2,128,1024]{3,1,2,0:T(2,128)(2,1)}), bf16[8,2,128,1024]{3,1,2,0:T(2,128)(2,1)}, u32[]{:S(2)}, u32[]{:S(2)}) async-start(bf16[8,2,128,1024]{3,1,2,0:T(2,128)(2,1)} %copy.28), calls=%async_computation.1 | async-start | bytes 8388608 | tf_op jit(solution)/shard_map/all_to_all | solution.py:43
  31.9 33.2 %collective-permute-done = bf16[1024,2048]{1,0:T(8,128)(2,1)} collective-permute-done((bf16[1024,2048]{1,0:T(8,128)(2,1)}, bf16[1024,2048]{1,0:T(8,128)(2,1)}, u32[]{:S(2)}, u32[]{:S(2)}) %collective-permute-start) | collective-permute-done | bytes 4194336 | tf_op jit(solution)/shard_map/ppermute | solution.py:12
  65.1 5.6 %convolution_convert_fusion = bf16[16,2048,128]{2,0,1:T(8,128)(2,1)S(1)} fusion(bf16[8,2048,128]{2,1,0:T(8,128)(2,1)} %param.10, s32[8]{0:T(128)S(1)} %fusion.29), kind=kOutput, calls=%fused_computation.12 | convolution fusion | flops 71303296 | bytes 12582944 | tf_op jit(solution)/shard_map/bs,bnd->snd/dot_general | solution.py:25
  70.7 7.1 %copy.31 = bf16[8,2,2048,128]{3,1,2,0:T(2,128)(2,1)} copy(bf16[8,2,2048,128]{3,1,0,2:T(2,128)(2,1)S(1)} %bitcast.39) | data formatting | bytes 16777216 | tf_op jit(solution)/shard_map/reshape | solution.py:38
  77.7 62.8 %all-to-all-done.1 = bf16[8,2,128,1024]{3,1,2,0:T(2,128)(2,1)} async-done(((bf16[8,2,128,1024]{3,1,2,0:T(2,128)(2,1)}), bf16[8,2,128,1024]{3,1,2,0:T(2,128)(2,1)}, u32[]{:S(2)}, u32[]{:S(2)}) %all-to-all-start.1) | async-done | bytes 4194336 | tf_op jit(solution)/shard_map/all_to_all | solution.py:43
  140.5 8.2 %all-to-all-start.2 = ((bf16[8,2,2048,128]{3,1,2,0:T(2,128)(2,1)}), bf16[8,2,2048,128]{3,1,2,0:T(2,128)(2,1)}, u32[]{:S(2)}, u32[]{:S(2)}) async-start(bf16[8,2,2048,128]{3,1,2,0:T(2,128)(2,1)} %copy.31), calls=%async_computation.2 | async-start | bytes 16777216 | tf_op jit(solution)/shard_map/all_to_all | solution.py:42
  148.7 37.8 %collective-permute-done.1 = bf16[1024,2048]{1,0:T(8,128)(2,1)} collective-permute-done((bf16[1024,2048]{1,0:T(8,128)(2,1)}, bf16[1024,2048]{1,0:T(8,128)(2,1)}, u32[]{:S(2)}, u32[]{:S(2)}) %collective-permute-start.1) | collective-permute-done | bytes 4194336 | tf_op jit(solution)/shard_map/ppermute | solution.py:12
  186.6 5.5 %copy.29 = bf16[8,2,128,1024]{3,2,1,0:T(8,128)(2,1)} copy(bf16[8,2,128,1024]{3,1,2,0:T(2,128)(2,1)} %all-to-all-done.1) | data formatting | bytes 8388608 | tf_op jit(solution)/shard_map/all_to_all | solution.py:43
  192.0 93.9 %all-to-all-done.2 = bf16[8,2,2048,128]{3,1,2,0:T(2,128)(2,1)} async-done(((bf16[8,2,2048,128]{3,1,2,0:T(2,128)(2,1)}), bf16[8,2,2048,128]{3,1,2,0:T(2,128)(2,1)}, u32[]{:S(2)}, u32[]{:S(2)}) %all-to-all-start.2) | async-done | bytes 8388640 | tf_op jit(solution)/shard_map/all_to_all | solution.py:42
  286.0 8.4 %copy.32 = bf16[8,2,2048,128]{3,2,1,0:T(8,128)(2,1)} copy(bf16[8,2,2048,128]{3,1,2,0:T(2,128)(2,1)} %all-to-all-done.2) | data formatting | bytes 16777216 | tf_op jit(solution)/shard_map/all_to_all | solution.py:42
  294.4 12.3 %pad_maximum_fusion = bf16[4,1024,2048]{2,1,0:T(8,128)(2,1)} fusion(bf16[1,1024,2048]{2,1,0:T(8,128)(2,1)} %bitcast.12, bf16[1,1024,2048]{2,1,0:T(8,128)(2,1)} %bitcast.11, bf16[1,1024,2048]{2,1,0:T(8,128)(2,1)} %bitcast.10, bf16[1,1024,2048]{2,1,0:T(8,128)(2,1)S(1)} %bitcast.42), kind=kLoop, calls=%fused_computation.11 | loop fusion | flops 25165824 | bytes 33554432 | tf_op jit(solution)/shard_map/stack | solution.py:52
  306.8 92.8 %while.13 = (s32[]{:T(128)}, f32[128,128]{1,0:T(8,128)S(1)}, s32[16]{0:T(128)S(1)}, bf16[16,128,1024]{2,1,0:T(8,128)(2,1)}, bf16[4,1024,2048]{2,1,0:T(8,128)(2,1...) while((s32[]{:T(128)}, f32[128,128]{1,0:T(8,128)S(1)}, s32[16]{0:T(128)S(1)}, ...), condition=%wide.region_5.6_spmd, body=%wide.region_2.5_spmd.sunk | while | flops 570572800 | bytes 5113027 | solution.py:71
  342.9 4.5 %conditional.2 = (f32[128,128]{1,0:T(8,128)S(1)}) conditional(s32[]{:T(128)} %convert_element_type.73, f32[128,128]{1,0:T(8,128)S(1)} %get-tuple-element.153, (bf16[16,128,1024]{2,1,0:T(8,128)(2,1)}, s32[]{:T(128)}, s32[]{:T(128)}, bf16[4,1024,2048]{2,1,0:T(8,128)(2,1)}, bf16[16,2048,128]{2,1,0:T(8,128)(2,1)}, ...), branch_computations={%region_3.3_spmd, %region_4.4_spmd} | conditional | flops 570572800 | bytes 5112868 | solution.py:68
  348.7 4.5 %conditional.2 = (f32[128,128]{1,0:T(8,128)S(1)}) conditional(s32[]{:T(128)} %convert_element_type.73, f32[128,128]{1,0:T(8,128)S(1)} %get-tuple-element.153, (bf16[16,128,1024]{2,1,0:T(8,128)(2,1)}, s32[]{:T(128)}, s32[]{:T(128)}, bf16[4,1024,2048]{2,1,0:T(8,128)(2,1)}, bf16[16,2048,128]{2,1,0:T(8,128)(2,1)}, ...), branch_computations={%region_3.3_spmd, %region_4.4_spmd} | conditional | flops 570572800 | bytes 5112868 | solution.py:68
  354.5 4.5 %conditional.2 = (f32[128,128]{1,0:T(8,128)S(1)}) conditional(s32[]{:T(128)} %convert_element_type.73, f32[128,128]{1,0:T(8,128)S(1)} %get-tuple-element.153, (bf16[16,128,1024]{2,1,0:T(8,128)(2,1)}, s32[]{:T(128)}, s32[]{:T(128)}, bf16[4,1024,2048]{2,1,0:T(8,128)(2,1)}, bf16[16,2048,128]{2,1,0:T(8,128)(2,1)}, ...), branch_computations={%region_3.3_spmd, %region_4.4_spmd} | conditional | flops 570572800 | bytes 5112868 | solution.py:68
  366.1 4.5 %conditional.2 = (f32[128,128]{1,0:T(8,128)S(1)}) conditional(s32[]{:T(128)} %convert_element_type.73, f32[128,128]{1,0:T(8,128)S(1)} %get-tuple-element.153, (bf16[16,128,1024]{2,1,0:T(8,128)(2,1)}, s32[]{:T(128)}, s32[]{:T(128)}, bf16[4,1024,2048]{2,1,0:T(8,128)(2,1)}, bf16[16,2048,128]{2,1,0:T(8,128)(2,1)}, ...), branch_computations={%region_3.3_spmd, %region_4.4_spmd} | conditional | flops 570572800 | bytes 5112868 | solution.py:68
  371.9 4.5 %conditional.2 = (f32[128,128]{1,0:T(8,128)S(1)}) conditional(s32[]{:T(128)} %convert_element_type.73, f32[128,128]{1,0:T(8,128)S(1)} %get-tuple-element.153, (bf16[16,128,1024]{2,1,0:T(8,128)(2,1)}, s32[]{:T(128)}, s32[]{:T(128)}, bf16[4,1024,2048]{2,1,0:T(8,128)(2,1)}, bf16[16,2048,128]{2,1,0:T(8,128)(2,1)}, ...), branch_computations={%region_3.3_spmd, %region_4.4_spmd} | conditional | flops 570572800 | bytes 5112868 | solution.py:68
  377.7 4.5 %conditional.2 = (f32[128,128]{1,0:T(8,128)S(1)}) conditional(s32[]{:T(128)} %convert_element_type.73, f32[128,128]{1,0:T(8,128)S(1)} %get-tuple-element.153, (bf16[16,128,1024]{2,1,0:T(8,128)(2,1)}, s32[]{:T(128)}, s32[]{:T(128)}, bf16[4,1024,2048]{2,1,0:T(8,128)(2,1)}, bf16[16,2048,128]{2,1,0:T(8,128)(2,1)}, ...), branch_computations={%region_3.3_spmd, %region_4.4_spmd} | conditional | flops 570572800 | bytes 5112868 | solution.py:68
  383.5 4.5 %conditional.2 = (f32[128,128]{1,0:T(8,128)S(1)}) conditional(s32[]{:T(128)} %convert_element_type.73, f32[128,128]{1,0:T(8,128)S(1)} %get-tuple-element.153, (bf16[16,128,1024]{2,1,0:T(8,128)(2,1)}, s32[]{:T(128)}, s32[]{:T(128)}, bf16[4,1024,2048]{2,1,0:T(8,128)(2,1)}, bf16[16,2048,128]{2,1,0:T(8,128)(2,1)}, ...), branch_computations={%region_3.3_spmd, %region_4.4_spmd} | conditional | flops 570572800 | bytes 5112868 | solution.py:68
  389.3 4.5 %conditional.2 = (f32[128,128]{1,0:T(8,128)S(1)}) conditional(s32[]{:T(128)} %convert_element_type.73, f32[128,128]{1,0:T(8,128)S(1)} %get-tuple-element.153, (bf16[16,128,1024]{2,1,0:T(8,128)(2,1)}, s32[]{:T(128)}, s32[]{:T(128)}, bf16[4,1024,2048]{2,1,0:T(8,128)(2,1)}, bf16[16,2048,128]{2,1,0:T(8,128)(2,1)}, ...), branch_computations={%region_3.3_spmd, %region_4.4_spmd} | conditional | flops 570572800 | bytes 5112868 | solution.py:68
  395.1 4.5 %conditional.2 = (f32[128,128]{1,0:T(8,128)S(1)}) conditional(s32[]{:T(128)} %convert_element_type.73, f32[128,128]{1,0:T(8,128)S(1)} %get-tuple-element.153, (bf16[16,128,1024]{2,1,0:T(8,128)(2,1)}, s32[]{:T(128)}, s32[]{:T(128)}, bf16[4,1024,2048]{2,1,0:T(8,128)(2,1)}, bf16[16,2048,128]{2,1,0:T(8,128)(2,1)}, ...), branch_computations={%region_3.3_spmd, %region_4.4_spmd} | conditional | flops 570572800 | bytes 5112868 | solution.py:68
  (61 shorter events, 112.3 us)
Async XLA Ops:
  0.0 8.8 %copy-start = (bf16[8,128,1024]{2,1,0:T(8,128)(2,1)S(1)}, bf16[8,128,1024]{2,1,0:T(8,128)(2,1)}, u32[]{:S(2)}) copy-start(bf16[8,128,1024]{2,1,0:T(8,128)(2,1)} %param.11) | copy-start | bytes 6291460
  0.0 65.1 %collective-permute-start = (bf16[1024,2048]{1,0:T(8,128)(2,1)}, bf16[1024,2048]{1,0:T(8,128)(2,1)}, u32[]{:S(2)}, u32[]{:S(2)}) collective-permute-start(bf16[1024,2048]{1,0:T(8,128)(2,1)} %param.9), channel_id=1, source_target_pairs={{0,8},{8,16},{16,24},{24,32},{32,40},{40,48},{48,56},{56,64},{64,7... | collective-permute-start | bytes 12582920 | tf_op jit(solution)/shard_map/ppermute | solution.py:12
  3.1 23.1 %all-to-all-start = ((bf16[8,1,2]{2,1,0:T(2,128)(2,1)}), bf16[8,1,2]{2,1,0:T(2,128)(2,1)S(1)}, u32[]{:S(2)}, u32[]{:S(2)}) async-start(bf16[8,1,2]{2,1,0:T(2,128)(2,1)} %convert_element_type.57), calls=%async_computation | async-start | bytes 8192 | tf_op jit(solution)/shard_map/all_to_all | solution.py:44
  26.2 114.3 %all-to-all-start.1 = ((bf16[8,2,128,1024]{3,1,2,0:T(2,128)(2,1)}), bf16[8,2,128,1024]{3,1,2,0:T(2,128)(2,1)}, u32[]{:S(2)}, u32[]{:S(2)}) async-start(bf16[8,2,128,1024]{3,1,2,0:T(2,128)(2,1)} %copy.28), calls=%async_computation.1 | async-start | bytes 8388608 | tf_op jit(solution)/shard_map/all_to_all | solution.py:43
  65.1 121.4 %collective-permute-start.1 = (bf16[1024,2048]{1,0:T(8,128)(2,1)}, bf16[1024,2048]{1,0:T(8,128)(2,1)}, u32[]{:S(2)}, u32[]{:S(2)}) collective-permute-start(bf16[1024,2048]{1,0:T(8,128)(2,1)} %collective-permute-done), channel_id=1, source_target_pairs={{0,8},{8,16},{16,24},{24,32},{32,40},{40,48},{48,56},{56,64},{64,7... | collective-permute-start | bytes 12582920 | tf_op jit(solution)/shard_map/ppermute | solution.py:12
  140.5 145.4 %all-to-all-start.2 = ((bf16[8,2,2048,128]{3,1,2,0:T(2,128)(2,1)}), bf16[8,2,2048,128]{3,1,2,0:T(2,128)(2,1)}, u32[]{:S(2)}, u32[]{:S(2)}) async-start(bf16[8,2,2048,128]{3,1,2,0:T(2,128)(2,1)} %copy.31), calls=%async_computation.2 | async-start | bytes 16777216 | tf_op jit(solution)/shard_map/all_to_all | solution.py:42
  186.5 107.9 %collective-permute-start.2 = (bf16[1024,2048]{1,0:T(8,128)(2,1)}, bf16[1024,2048]{1,0:T(8,128)(2,1)}, u32[]{:S(2)}, u32[]{:S(2)}) collective-permute-start(bf16[1024,2048]{1,0:T(8,128)(2,1)} %collective-permute-done.1), channel_id=1, source_target_pairs={{0,8},{8,16},{16,24},{24,32},{32,40},{40,48},{48,56},{56,64},{64,7... | collective-permute-start | bytes 12582920 | tf_op jit(solution)/shard_map/ppermute | solution.py:12
  286.0 8.5 %copy-start.2 = (bf16[1024,2048]{1,0:T(8,128)(2,1)S(1)}, bf16[1024,2048]{1,0:T(8,128)(2,1)}, u32[]{:S(2)}) copy-start(bf16[1024,2048]{1,0:T(8,128)(2,1)} %param.9) | copy-start | bytes 12582916
  399.6 0.6 copy-start.3
  400.3 1.6 copy-start.1
where the time goes:
time: 403 us; the launch traced here: 402 us
  waiting for transfers between devices  228 us (57%)
  matrix products  70.6 us (18%)
  local copies, waits for them, and re-layouts  48.5 us (12%)
  loops' own time  20.7 us (5%)
  starting transfers between devices  19.6 us (5%)
  other arithmetic  14.8 us (4%)
    all_to_all x1, waiting for transfers between devices, body(): lax.all_to_all(packed_weight, 'tile', split_axis=0, concat_axis=0, tiled=...  93.9 us
    ppermute x3, waiting for transfers between devices, from_behind(): lax.ppermute(array, axis, [(i, (i + by) % count) for i in range(count)])  71 us
    all_to_all x1, waiting for transfers between devices, body(): lax.all_to_all(packed_amplitude, 'tile', split_axis=0, concat_axis=0, til...  62.8 us
    dot_general x16, matrix products, filled(): jnp.dot(amplitude, projected, preferred_element_type=jnp.float32)  61.9 us
    reshape x2, local copies, waits for them, and re-layouts, body(): packed_amplitude.reshape(tiles_count, MOST, lateral_count, trace_count)  14.2 us
    another operation x1, other arithmetic, body(): stacked = jnp.stack(visits)  12.3 us
    another operation x1, loops' own time, body(): lax.scan(spray, image_sum, (got_weight, got_amplitude, got_code))  10.4 us
    dynamic_slice x16, local copies, waits for them, and re-layouts, body(): lax.scan(spray, image_sum, (got_weight, got_amplitude, got_code))  10.3 us
  transfers between devices with their start and end apart: 6, of which 4 were waited for; matrix products, arithmetic and copies ran while one was open for 12% of the time, Pallas kernels for 0%

commit v1 on v0

v1 whole, which is shorter than its diff:
```python
import jax
import jax.numpy as jnp
from jax import lax
from jax.experimental import pallas as pl
from jax.experimental.pallas import tpu as pltpu
from jax.sharding import PartitionSpec as P

MESH = pl.DeviceIdType.MESH
MOST = 2
STOPS = 4
UPPER = 64
PIECES = 4
OFFSETS = (2, 1, 3)
CHUNK = 256
F32 = jnp.float32
BF16 = jnp.bfloat16


def kernel(r_hbm, w_hbm, a_hbm, tile_ref, stop_ref, out_ref, r_all, a_own, w_own, a_pair, w_pair, sa_own, sw_own, sa_pair,
           sw_pair, d_a, d_w, d_info, s_own, s_all, acc, part, loc, info_s, info_r, r_s, r_r, az_s, az_r, wz_s, wz_r,
           ap_s, ap_r, wp_s, wp_r, apz_s, apz_r, wpz_s, wpz_r, al_s, al_r, o_s, o_r):
    blk, tile = lax.axis_index("blk"), lax.axis_index("tile")
    groups, tiles = lax.axis_size("blk"), lax.axis_size("tile")
    zs = tiles // 2
    core, yh = blk % 2, (blk // 2) % 2
    z, h = tile // 2, tile % 2
    label = (h + yh) % 2
    blocks, lat = a_own.shape[0], a_own.shape[1]
    half = w_own.shape[1]
    rows = half // PIECES
    mine = pl.ds(pl.multiple_of(label * half, half), half)
    other = pl.ds(pl.multiple_of((1 - label) * half, half), half)

    pair = (blk, z * 2 + 1 - h)
    sibling = (blk + 1 - 2 * core, tile)
    next_chip = ((blk + 2) % groups, z * 2 + 1 - h)
    after_next = ((blk + 3) % groups, tile)
    drop = ((blk + groups - 1) % groups, z * 2 + 1 - h)
    is_b = (yh * core) == 0
    is_c = core == 1
    is_d = (yh * (1 - core)) == 1

    def remote(src, dst, send, recv, where):
        return pltpu.make_async_remote_copy(src_ref=src, dst_ref=dst, send_sem=send, recv_sem=recv, device_id=where,
                                            device_id_type=MESH)

    def lane_of(d):
        return (blk, ((z + d) % zs) * 2 + h)

    barrier = pltpu.get_barrier_semaphore()

    def greet(where):
        pl.semaphore_signal(barrier, inc=1, device_id=where, device_id_type=MESH)

    for j in range(1, 8):
        greet((blk, (tile + j) % tiles))
    greet(sibling)
    from_yh0_odd = (yh == 0) & (core == 1)

    @pl.when(from_yh0_odd)
    def _():
        greet(((blk + 1) % groups, z * 2 + 1 - h))

    @pl.when(jnp.logical_not(from_yh0_odd))
    def _():
        greet(((blk + groups - 2) % groups, z * 2 + 1 - h))

    @pl.when(core == 0)
    def _():
        greet(((blk + groups - 3) % groups, tile))

    lane = lax.broadcasted_iota(jnp.int32, d_info.shape[1:], 1)
    line = lax.broadcasted_iota(jnp.int32, d_info.shape[1:], 0)
    info = jnp.zeros(d_info.shape[1:], jnp.int32)
    targets = [tile_ref[b, 0] for b in range(blocks)]
    for b in range(blocks):
        rank = sum([(targets[e] == targets[b]).astype(jnp.int32) for e in range(b)], jnp.int32(0))
        value = jnp.where(line == 0, b, jnp.where(line == 1, stop_ref[b], 1))
        info = jnp.where(lane == targets[b] * MOST + rank, value, info)
    d_info[tile] = info

    cp_own = pltpu.make_async_copy(d_info.at[tile], s_own, loc.at[0])
    cp_own.start()
    cp_r = pltpu.make_async_copy(r_hbm.at[:, mine], r_all.at[h, 0], loc.at[1])
    cp_a = pltpu.make_async_copy(a_hbm, a_own, loc.at[2])
    cp_w = pltpu.make_async_copy(w_hbm.at[:, mine, :], w_own, loc.at[3])
    cp_r.start()
    cp_a.start()
    cp_w.start()

    pl.semaphore_wait(barrier, 8 + (1 - yh * core) + core + yh * (1 - core))

    def info_copy(j):
        return remote(d_info.at[tile], d_info.at[tile], info_s.at[j], info_r.at[j], (blk, (tile + j) % tiles))

    for j in range(1, 8):
        info_copy(j).start()

    r_pair = remote(r_hbm.at[:, other], r_all.at[h, 0], r_s.at[0, 0], r_r.at[h, 0], pair)
    a_over = remote(a_hbm.at[:, 0:UPPER, :], a_pair, ap_s.at[0], ap_r.at[0], pair)

    def w_over(i):
        at = pl.ds(pl.multiple_of((1 - label) * half + i * rows, rows), rows)
        return remote(w_hbm.at[:, at, :], w_pair[i], wp_s.at[i], wp_r.at[i], pair)

    r_pair.start()
    a_over.start()
    for i in range(PIECES):
        w_over(i).start()

    def hop(op, j, tau, k_from, k_to, where):
        return remote(r_all.at[tau, k_from], r_all.at[tau, k_to], r_s.at[op, j], r_r.at[tau, k_to], where)

    def taus(j):
        return h if j == 0 else 1 - h

    def op_a(j):
        return hop(1, j, taus(j), 0, 1, sibling)

    def op_b(j):
        return hop(2, j, taus(j), 0, 2, next_chip)

    def op_c(j):
        return hop(3, j, taus(j), 0, 3, after_next)

    def op_d(j):
        return hop(4, j, taus(j), 3, 2, drop)

    def op_e0(j):
        return hop(5, j, taus(j), 2, 3, sibling)

    def op_e1(j):
        return hop(5, j, taus(j), 2, 1, sibling)

    def got_r(tau, k):
        remote(r_all.at[tau, k], r_all.at[tau, k], r_s.at[0, 0], r_r.at[tau, k], pair).wait_recv()

    def spread(j):
        @pl.when(is_c)
        def _():
            op_c(j).start()

        @pl.when(is_b)
        def _():
            op_b(j).start()

        @pl.when(core == 0)
        def _():
            op_a(j).start()

    def forward(j):
        got_r(taus(j), 2)

        @pl.when(core == 0)
        def _():
            op_e0(j).start()

        @pl.when(core == 1)
        def _():
            op_e1(j).start()

    def arrive_3(j):
        got_r(taus(j), 3)

        @pl.when(is_d)
        def _():
            op_d(j).start()

    cp_r.wait()
    spread(0)

    src_me = tile
    src_pair = z * 2 + 1 - h

    def pack(table, count, base, load, store):
        def one(r, carry):
            store(r, load(table(base + r)))
            return carry

        lax.fori_loop(0, count, one, 0)

    def own_block(slot):
        return s_own[0, slot]

    def pair_block(slot):
        return s_all[src_pair, 0, slot]

    def base_of(d):
        return ((z + d) % zs) * (2 * MOST)

    def a_out(d):
        return remote(sa_own.at[d - 1], d_a.at[src_me], az_s.at[d - 1], az_r.at[d - 1], lane_of(d))

    def w_out(d):
        return remote(sw_own.at[d - 1], d_w.at[src_me], wz_s.at[d - 1], wz_r.at[d - 1], lane_of(d))

    cp_own.wait()
    cp_a.wait()
    for d in OFFSETS:
        def put(r, value, d=d):
            sa_own[d - 1, r] = value

        pack(own_block, 4, base_of(d), lambda b: a_own[b], put)
        a_out(d).start()

    def put_a(r, value):
        d_a[src_me, r] = value

    pack(own_block, 4, base_of(0), lambda b: a_own[b], put_a)

    def low(d):
        src = ((z + zs - d) % zs) * 2 + h
        return remote(d_a.at[src, :, UPPER:lat, :], d_a.at[src, :, UPPER:lat, :], al_s.at[d], al_r.at[d], pair)

    low(0).start()
    cp_w.wait()
    for d in OFFSETS:
        def put(r, value, d=d):
            sw_own[d - 1, r] = value

        pack(own_block, 4, base_of(d), lambda b: w_own[b], put)
        w_out(d).start()

    def put_w(r, value):
        d_w[src_me, r] = value

    pack(own_block, 4, base_of(0), lambda b: w_own[b], put_w)

    for j in range(1, 8):
        src = (tile + tiles - j) % tiles
        remote(d_info.at[src], d_info.at[src], info_s.at[j], info_r.at[j], pair).wait_recv()
    cp_all = pltpu.make_async_copy(d_info, s_all, loc.at[4])
    cp_all.start()
    cp_all.wait()

    got_r(1 - h, 0)
    spread(1)

    def ap_out(d):
        return remote(sa_pair.at[d - 1], d_a.at[src_pair, :, 0:UPPER, :], apz_s.at[d - 1], apz_r.at[d - 1], lane_of(d))

    def wp_out(i, d):
        return remote(sw_pair.at[i, d - 1], d_w.at[src_pair, :, pl.ds(i * rows, rows), :], wpz_s.at[i, d - 1],
                      wpz_r.at[i, d - 1], lane_of(d))

    a_over.wait_recv()
    for d in OFFSETS:
        def put(r, value, d=d):
            sa_pair[d - 1, r] = value

        pack(pair_block, 4, base_of(d), lambda b: a_pair[b], put)
        ap_out(d).start()

    def put_ap(r, value):
        d_a[src_pair, r, 0:UPPER, :] = value

    pack(pair_block, 4, base_of(0), lambda b: a_pair[b], put_ap)

    def relay_piece(i):
        w_over(i).wait_recv()
        for d in OFFSETS:
            def put(r, value, d=d):
                sw_pair[i, d - 1, r] = value

            pack(pair_block, 4, base_of(d), lambda b: w_pair[i][b], put)
            wp_out(i, d).start()

        def put_wp(r, value):
            d_w[src_pair, r, i * rows:(i + 1) * rows, :] = value

        pack(pair_block, 4, base_of(0), lambda b: w_pair[i][b], put_wp)

    def source(d, flip):
        return ((z + zs - d) % zs) * 2 + (1 - h if flip else h)

    def got_own_a(d):
        src = source(d, False)
        remote(d_a.at[src], d_a.at[src], az_s.at[d - 1], az_r.at[d - 1], pair).wait_recv()

    for d in (1, 3, 2):
        got_own_a(d)
        low(d).start()

    @pl.when(core == 0)
    def _():
        arrive_3(0)

    forward(1)
    relay_piece(0)
    relay_piece(1)

    @pl.when(core == 0)
    def _():
        arrive_3(1)

    forward(0)
    relay_piece(2)
    relay_piece(3)

    got_r(0, 1)
    got_r(1, 1)

    @pl.when(core == 1)
    def _():
        got_r(0, 3)
        got_r(1, 3)

    acc[...] = jnp.zeros_like(acc)
    first = z * (2 * MOST)

    def facts(src, r):
        return s_all[src, 1, first + r], s_all[src, 2, first + r].astype(F32)

    def chunk_q(src, r, k, n):
        return jnp.dot(d_a[src, r], r_all[r // MOST, k, :, n * CHUNK:(n + 1) * CHUNK],
                       preferred_element_type=F32).astype(BF16)

    def whole(src):
        def one(r, carry):
            k, filled = facts(src, r)
            total = jnp.zeros(acc.shape[1:], F32)
            for n in range(half // CHUNK):
                total += jnp.dot(chunk_q(src, r, k, n), d_w[src, r, n * CHUNK:(n + 1) * CHUNK, :],
                                 preferred_element_type=F32)
            acc[r // MOST] += filled * total
            return carry

        lax.fori_loop(0, 2 * MOST, one, 0)

    def front(src, d):
        def one(r, carry):
            k, _ = facts(src, r)
            for n in range(half // CHUNK):
                sa_own[d - 1, r, :, n * CHUNK:(n + 1) * CHUNK] = chunk_q(src, r, k, n)
            return carry

        lax.fori_loop(0, 2 * MOST, one, 0)

    def back(src, d):
        def one(r, carry):
            _, filled = facts(src, r)
            acc[r // MOST] += filled * jnp.dot(sa_own[d - 1, r], d_w[src, r], preferred_element_type=F32)
            return carry

        lax.fori_loop(0, 2 * MOST, one, 0)

    whole(src_me)
    for d in (1, 3, 2):
        src = source(d, False)
        remote(d_w.at[src], d_w.at[src], wz_s.at[d - 1], wz_r.at[d - 1], pair).wait_recv()
        whole(src)

    def got_low(d):
        at = d_a.at[source(d, True), :, UPPER:lat, :]
        remote(at, at, al_s.at[d], al_r.at[d], pair).wait_recv()

    got_low(0)
    whole(src_pair)
    for d in OFFSETS:
        a_out(d).wait_send()
    for d in (1, 3, 2):
        src = source(d, True)
        at = d_a.at[src, :, 0:UPPER, :]
        remote(at, at, apz_s.at[d - 1], apz_r.at[d - 1], pair).wait_recv()
        got_low(d)
        front(src, d)
    for d in (1, 3, 2):
        src = source(d, True)
        for i in range(PIECES):
            at = d_w.at[src, :, pl.ds(i * rows, rows), :]
            remote(at, at, wpz_s.at[i, d - 1], wpz_r.at[i, d - 1], pair).wait_recv()
        back(src, d)

    home = remote(acc.at[1 - h], part, o_s.at[0], o_r.at[0], pair)
    home.start()

    for j in range(1, 8):
        info_copy(j).wait_send()
    r_pair.wait_send()
    a_over.wait_send()
    for i in range(PIECES):
        w_over(i).wait_send()
    for d in OFFSETS:
        w_out(d).wait_send()
        ap_out(d).wait_send()
        for i in range(PIECES):
            wp_out(i, d).wait_send()
    for d in range(4):
        low(d).wait_send()
    for j in range(2):
        @pl.when(is_c)
        def _():
            op_c(j).wait_send()

        @pl.when(is_b)
        def _():
            op_b(j).wait_send()

        @pl.when(is_d)
        def _():
            op_d(j).wait_send()

        @pl.when(core == 0)
        def _():
            op_a(j).wait_send()
            op_e0(j).wait_send()

        @pl.when(core == 1)
        def _():
            op_e1(j).wait_send()

    home.wait()
    out_ref[...] = acc[h] + part[...]


def body(residual_traces, time_weights, lateral_amplitude, intersection_tile, visit_stop):
    traces, samples = residual_traces.shape
    blocks, _, depth = time_weights.shape
    lat = lateral_amplitude.shape[1]
    tiles = lax.axis_size("tile")
    half, slots = samples // 2, 2 * MOST
    rows = half // PIECES
    hops = tiles // 2 - 1
    dma = pltpu.SemaphoreType.DMA
    return pl.pallas_call(
        kernel,
        out_shape=jax.ShapeDtypeStruct((lat, depth), F32),
        in_specs=[pl.BlockSpec(memory_space=pl.ANY)] * 3 + [pl.BlockSpec(memory_space=pltpu.SMEM)] * 2,
        out_specs=pl.BlockSpec(memory_space=pltpu.VMEM),
        scratch_shapes=[
            pltpu.VMEM((2, STOPS, traces, half), BF16),
            pltpu.VMEM((blocks, lat, traces), BF16),
            pltpu.VMEM((blocks, half, depth), BF16),
            pltpu.VMEM((blocks, UPPER, traces), BF16),
            [pltpu.VMEM((blocks, rows, depth), BF16)] * PIECES,
            pltpu.VMEM((hops, slots, lat, traces), BF16),
            pltpu.VMEM((hops, slots, half, depth), BF16),
            pltpu.VMEM((hops, slots, UPPER, traces), BF16),
            pltpu.VMEM((PIECES, hops, slots, rows, depth), BF16),
            pltpu.VMEM((tiles, slots, lat, traces), BF16),
            pltpu.VMEM((tiles, slots, half, depth), BF16),
            pltpu.VMEM((tiles, 8, 128), jnp.int32),
            pltpu.SMEM((8, 128), jnp.int32),
            pltpu.SMEM((tiles, 8, 128), jnp.int32),
            pltpu.VMEM((2, lat, depth), F32),
            pltpu.VMEM((lat, depth), F32),
            dma((5,)), dma((8,)), dma((8,)), dma((6, 2)), dma((2, STOPS)),
            dma((hops,)), dma((hops,)), dma((hops,)), dma((hops,)), dma((1,)), dma((1,)),
            dma((PIECES,)), dma((PIECES,)), dma((hops,)), dma((hops,)), dma((PIECES, hops)), dma((PIECES, hops)),
            dma((4,)), dma((4,)), dma((1,)), dma((1,)),
        ],
        compiler_params=pltpu.CompilerParams(collective_id=0, has_side_effects=True, vmem_limit_bytes=60 << 20),
        cost_estimate=pl.CostEstimate(flops=10 << 30, bytes_accessed=12 << 20, transcendentals=0),
    )(residual_traces, time_weights, lateral_amplitude, intersection_tile, visit_stop)


def solution(mesh):
    assert mesh.shape["blk"] == 16 and mesh.shape["tile"] == 8
    in_specs = (
        P(("blk", "tile"), None),
        P(("blk", "tile"), None, None),
        P(("blk", "tile"), None, None),
        P(("blk", "tile"), None),
        P(("blk", "tile")),
    )
    out_specs = P(("blk", "tile"), None)
    return jax.shard_map(body, mesh=mesh, in_specs=in_specs, out_specs=out_specs, check_vma=False)
```

time: 403 us -> 177 us (0.44)
  waiting for transfers between devices: 228 us -> 0 us
  Pallas kernels: 0 us -> 172 us
  matrix products: 70.6 us -> 0 us
  local copies, waits for them, and re-layouts: 48.5 us -> 2.79 us
  loops' own time: 20.7 us -> 0 us
  starting transfers between devices: 19.6 us -> 0 us
  other arithmetic: 14.8 us -> 0 us
    pallas_call x0 -> x1, Pallas kernels: none -> 172 us  [body(): pl.pallas_call(kernel, out_shape=jax.ShapeDtypeStruct((lat, depth), F32),...]
    all_to_all x3 -> x0, waiting for transfers between devices: 157 us -> none  [the longest x1 93.9 us: body(): lax.all_to_all(packed_weight, 'tile', split_axis=0, concat_axis=0, tiled=...]
    ppermute x3 -> x0, waiting for transfers between devices: 71 us -> none  [from_behind(): lax.ppermute(array, axis, [(i, (i + by) % count) for i in range(count)])]
    dot_general x18 -> x0, matrix products: 70.6 us -> none  [the longest x16 61.9 us: filled(): jnp.dot(amplitude, projected, preferred_element_type=jnp.float32)]
    reshape x3 -> x0, local copies, waits for them, and re-layouts: 21.3 us -> none  [the longest x2 14.2 us: body(): packed_amplitude.reshape(tiles_count, MOST, lateral_count, trace_count)]
    another operation x17 -> x0, loops' own time: 20.7 us -> none  [the longest x1 10.4 us: body(): lax.scan(spray, image_sum, (got_weight, got_amplitude, got_code))]
    all_to_all x3 -> x0, starting transfers between devices: 19.6 us -> none  [the longest x1 8.16 us: body(): lax.all_to_all(packed_weight, 'tile', split_axis=0, concat_axis=0, tiled=...]
    all_to_all x2 -> x0, local copies, waits for them, and re-layouts: 13.9 us -> none  [the longest x1 8.44 us: body(): lax.all_to_all(packed_weight, 'tile', split_axis=0, concat_axis=0, tiled=...]
  transfers between devices with their start and end apart: 6 -> 0, of which waited for: 4 -> 0; matrix products, arithmetic and copies ran while one was open for 12% -> 0% of each run, Pallas kernels for 0% -> 0%
where the time goes in v1:
time: 177 us; the launch traced here: 174 us
  Pallas kernels  172 us (97%)
  local copies, waits for them, and re-layouts  2.79 us (2%)
    pallas_call x1, Pallas kernels, body(): pl.pallas_call(kernel, out_shape=jax.ShapeDtypeStruct((lat, depth), F32),...  172 us

profile of v1, /device:TPU:80, one launch (start us, length us, event | category | flops | bytes accessed | tf_op | source)
XLA Modules:
  0.0 174.4 jit_solution(18242931950989996518)
XLA Ops:
  0.0 1.3 copy.6.tile_ref
  1.3 171.6 %shard_map.55 = f32[128,128]{1,0:T(8,128)} custom-call(bf16[1024,2048]{1,0:T(8,128)(2,1)} %r_hbm.1, bf16[8,2048,128]{2,1,0:T(8,128)(2,1)} %w_hbm.1, bf16[8,128,1024]{2,1,0:T(8,128)(2,1)} %a_hbm.1, s32[8,1]{1,0:T(8,128)} %copy.6.tile_ref, s32[8]{0:T(128)} %stop_ref.1), custom_call_target="tpu_custom_call" | custom-call | flops 10737418240 | bytes 12582912 | tf_op jit(solution)/shard_map/pallas_call | solution.py:425
  172.9 1.5 copy.8

commit v2 on v1

v2 whole, which is shorter than its diff:
```python
import jax
import jax.numpy as jnp
from jax import lax
from jax.experimental import pallas as pl
from jax.experimental.pallas import tpu as pltpu
from jax.sharding import PartitionSpec as P

MESH = pl.DeviceIdType.MESH
MOST = 2
STOPS = 4
UPPER = 64
PIECES = 4
OFFSETS = (2, 1, 3)
CHUNK = 512
F32 = jnp.float32
BF16 = jnp.bfloat16


def kernel(r_hbm, w_hbm, a_hbm, tile_ref, stop_ref, out_ref, r_all, a_own, w_own, a_pair, w_pair, sa_own, sw_own, sa_pair,
           sw_pair, d_a, d_w, d_info, s_all, acc, part, loc, info_s, info_r, r_s, r_r, az_s, az_r, wz_s, wz_r,
           ap_s, ap_r, wp_s, wp_r, apz_s, apz_r, wpz_s, wpz_r, al_s, al_r, o_s, o_r):
    blk, tile = lax.axis_index("blk"), lax.axis_index("tile")
    groups, tiles = lax.axis_size("blk"), lax.axis_size("tile")
    zs = tiles // 2
    core, yh = blk % 2, (blk // 2) % 2
    z, h = tile // 2, tile % 2
    label = (h + yh) % 2
    blocks, lat = a_own.shape[0], a_own.shape[1]
    half = w_own.shape[1]
    rows = half // PIECES
    mine = pl.ds(pl.multiple_of(label * half, half), half)
    other = pl.ds(pl.multiple_of((1 - label) * half, half), half)

    pair = (blk, z * 2 + 1 - h)
    sibling = (blk + 1 - 2 * core, tile)
    next_chip = ((blk + 2) % groups, z * 2 + 1 - h)
    after_next = ((blk + 3) % groups, tile)
    drop = ((blk + groups - 1) % groups, z * 2 + 1 - h)
    is_b = (yh * core) == 0
    is_c = core == 1
    is_d = (yh * (1 - core)) == 1

    def remote(src, dst, send, recv, where):
        return pltpu.make_async_remote_copy(src_ref=src, dst_ref=dst, send_sem=send, recv_sem=recv, device_id=where,
                                            device_id_type=MESH)

    def lane_of(d):
        return (blk, ((z + d) % zs) * 2 + h)

    cp_a = pltpu.make_async_copy(a_hbm, a_own, loc.at[0])
    cp_r = pltpu.make_async_copy(r_hbm.at[:, mine], r_all.at[h, 0], loc.at[1])
    cp_w = pltpu.make_async_copy(w_hbm.at[:, mine, :], w_own, loc.at[2])
    cp_a.start()
    cp_r.start()
    cp_w.start()

    barrier = pltpu.get_barrier_semaphore()

    def greet(where):
        pl.semaphore_signal(barrier, inc=1, device_id=where, device_id_type=MESH)

    for j in range(1, 8):
        greet((blk, (tile + j) % tiles))
    greet(sibling)
    from_yh0_odd = (yh == 0) & (core == 1)

    @pl.when(from_yh0_odd)
    def _():
        greet(((blk + 1) % groups, z * 2 + 1 - h))

    @pl.when(jnp.logical_not(from_yh0_odd))
    def _():
        greet(((blk + groups - 2) % groups, z * 2 + 1 - h))

    @pl.when(core == 0)
    def _():
        greet(((blk + groups - 3) % groups, tile))

    lane = lax.broadcasted_iota(jnp.int32, d_info.shape[1:], 1)
    line = lax.broadcasted_iota(jnp.int32, d_info.shape[1:], 0)
    info = jnp.zeros(d_info.shape[1:], jnp.int32)
    targets = [tile_ref[b] for b in range(blocks)]
    slot_of = []
    for b in range(blocks):
        rank = sum([(targets[e] == targets[b]).astype(jnp.int32) for e in range(b)], jnp.int32(0))
        slot_of.append(targets[b] * MOST + rank)
        value = jnp.where(line == 0, b, jnp.where(line == 1, stop_ref[b], 1))
        info = jnp.where(lane == slot_of[b], value, info)
    d_info[tile] = info

    src_me = tile
    src_pair = z * 2 + 1 - h

    def pack(table, count, base, load, store):
        def one(r, carry):
            store(r, load(table(base + r)))
            return carry

        lax.fori_loop(0, count, one, 0)

    def own_block(slot):
        block = jnp.int32(0)
        for b in range(1, blocks):
            block = jnp.where(slot_of[b] == slot, b, block)
        return block

    def pair_block(slot):
        return s_all[src_pair, 0, slot]

    def base_of(d):
        return ((z + d) % zs) * (2 * MOST)

    def a_out(d):
        return remote(sa_own.at[d - 1], d_a.at[src_me], az_s.at[d - 1], az_r.at[d - 1], lane_of(d))

    cp_a.wait()
    for d in OFFSETS:
        def put(r, value, d=d):
            sa_own[d - 1, r] = value

        pack(own_block, 4, base_of(d), lambda b: a_own[b], put)

    pl.semaphore_wait(barrier, 8 + (1 - yh * core) + core + yh * (1 - core))

    def info_copy(j):
        return remote(d_info.at[tile], d_info.at[tile], info_s.at[j], info_r.at[j], (blk, (tile + j) % tiles))

    for j in range(1, 8):
        info_copy(j).start()

    r_pair = remote(r_hbm.at[:, other], r_all.at[h, 0], r_s.at[0, 0], r_r.at[h, 0], pair)
    a_over = remote(a_hbm.at[:, 0:UPPER, :], a_pair, ap_s.at[0], ap_r.at[0], pair)

    def w_over(i):
        at = pl.ds(pl.multiple_of((1 - label) * half + i * rows, rows), rows)
        return remote(w_hbm.at[:, at, :], w_pair[i], wp_s.at[i], wp_r.at[i], pair)

    r_pair.start()
    for d in OFFSETS:
        a_out(d).start()
    a_over.start()
    for i in range(PIECES):
        w_over(i).start()

    def hop(op, j, tau, k_from, k_to, where):
        return remote(r_all.at[tau, k_from], r_all.at[tau, k_to], r_s.at[op, j], r_r.at[tau, k_to], where)

    def taus(j):
        return h if j == 0 else 1 - h

    def op_a(j):
        return hop(1, j, taus(j), 0, 1, sibling)

    def op_b(j):
        return hop(2, j, taus(j), 0, 2, next_chip)

    def op_c(j):
        return hop(3, j, taus(j), 0, 3, after_next)

    def op_d(j):
        return hop(4, j, taus(j), 3, 2, drop)

    def op_e0(j):
        return hop(5, j, taus(j), 2, 3, sibling)

    def op_e1(j):
        return hop(5, j, taus(j), 2, 1, sibling)

    def got_r(tau, k):
        remote(r_all.at[tau, k], r_all.at[tau, k], r_s.at[0, 0], r_r.at[tau, k], pair).wait_recv()

    def spread(j):
        @pl.when(is_c)
        def _():
            op_c(j).start()

        @pl.when(is_b)
        def _():
            op_b(j).start()

        @pl.when(core == 0)
        def _():
            op_a(j).start()

    def forward(j):
        got_r(taus(j), 2)

        @pl.when(core == 0)
        def _():
            op_e0(j).start()

        @pl.when(core == 1)
        def _():
            op_e1(j).start()

    def arrive_3(j):
        got_r(taus(j), 3)

        @pl.when(is_d)
        def _():
            op_d(j).start()

    cp_r.wait()
    spread(0)

    def w_out(d):
        return remote(sw_own.at[d - 1], d_w.at[src_me], wz_s.at[d - 1], wz_r.at[d - 1], lane_of(d))

    def put_a(r, value):
        d_a[src_me, r] = value

    pack(own_block, 4, base_of(0), lambda b: a_own[b], put_a)

    def source(d, flip):
        return ((z + zs - d) % zs) * 2 + (1 - h if flip else h)

    def low_at(src, tau):
        return d_a.at[src, pl.ds(tau * MOST, MOST), UPPER:lat, :]

    def low(d, t):
        at = low_at(source(d, False), h if t == 0 else 1 - h)
        return remote(at, at, al_s.at[d, t], al_r.at[d, t], pair)

    cp_w.wait()
    for d in OFFSETS:
        def put(r, value, d=d):
            sw_own[d - 1, r] = value

        pack(own_block, 4, base_of(d), lambda b: w_own[b], put)
        w_out(d).start()

    def put_w(r, value):
        d_w[src_me, r] = value

    pack(own_block, 4, base_of(0), lambda b: w_own[b], put_w)

    for j in range(1, 8):
        src = (tile + tiles - j) % tiles
        remote(d_info.at[src], d_info.at[src], info_s.at[j], info_r.at[j], pair).wait_recv()
    cp_all = pltpu.make_async_copy(d_info, s_all, loc.at[3])
    cp_all.start()
    cp_all.wait()

    got_r(1 - h, 0)
    spread(1)

    def ap_out(d):
        return remote(sa_pair.at[d - 1], d_a.at[src_pair, :, 0:UPPER, :], apz_s.at[d - 1], apz_r.at[d - 1], lane_of(d))

    def wp_out(i, d, t):
        two = pl.ds((1 - h if t == 0 else h) * MOST, MOST)
        return remote(sw_pair.at[i, d - 1, two], d_w.at[src_pair, two, pl.ds(i * rows, rows), :], wpz_s.at[i, d - 1, t],
                      wpz_r.at[i, d - 1, t], lane_of(d))

    a_over.wait_recv()
    for d in OFFSETS:
        def put(r, value, d=d):
            sa_pair[d - 1, r] = value

        pack(pair_block, 4, base_of(d), lambda b: a_pair[b], put)
        ap_out(d).start()

    def put_ap(r, value):
        d_a[src_pair, r, 0:UPPER, :] = value

    pack(pair_block, 4, base_of(0), lambda b: a_pair[b], put_ap)

    def relay_piece(i, t):
        skip = (1 - h if t == 0 else h) * MOST
        for d in OFFSETS:
            def put(r, value, d=d):
                sw_pair[i, d - 1, skip + r] = value

            pack(pair_block, MOST, base_of(d) + skip, lambda b: w_pair[i][b], put)
            wp_out(i, d, t).start()

        def put_wp(r, value):
            d_w[src_pair, skip + r, i * rows:(i + 1) * rows, :] = value

        pack(pair_block, MOST, base_of(0) + skip, lambda b: w_pair[i][b], put_wp)

    def got_own_a(d):
        src = source(d, False)
        remote(d_a.at[src], d_a.at[src], az_s.at[d - 1], az_r.at[d - 1], pair).wait_recv()

    for d in (1, 3, 2):
        got_own_a(d)
    for t in range(2):
        for d in range(4):
            low(d, t).start()

    @pl.when(core == 0)
    def _():
        arrive_3(0)

    forward(1)
    w_over(0).wait_recv()
    relay_piece(0, 0)
    w_over(1).wait_recv()
    relay_piece(1, 0)

    @pl.when(core == 0)
    def _():
        arrive_3(1)

    w_over(2).wait_recv()
    relay_piece(2, 0)
    w_over(3).wait_recv()
    relay_piece(3, 0)
    for i in range(PIECES):
        relay_piece(i, 1)
    forward(0)

    got_r(0, 1)
    got_r(1, 1)

    @pl.when(core == 1)
    def _():
        got_r(0, 3)
        got_r(1, 3)

    acc[...] = jnp.zeros_like(acc)
    first = z * (2 * MOST)

    def facts(src, r):
        return s_all[src, 1, first + r], s_all[src, 2, first + r].astype(F32)

    def chunk_q(src, r, k, n):
        return jnp.dot(d_a[src, r], r_all[r // MOST, k, :, n * CHUNK:(n + 1) * CHUNK],
                       preferred_element_type=F32).astype(BF16)

    def whole(src, begin, count):
        def one(r, carry):
            k, filled = facts(src, r)
            total = jnp.zeros(acc.shape[1:], F32)
            for n in range(half // CHUNK):
                total += jnp.dot(chunk_q(src, r, k, n), d_w[src, r, n * CHUNK:(n + 1) * CHUNK, :],
                                 preferred_element_type=F32)
            acc[r // MOST] += filled * total
            return carry

        lax.fori_loop(begin, begin + count, one, 0)

    def front(src, d, begin):
        def one(r, carry):
            k, _ = facts(src, r)
            for n in range(half // CHUNK):
                sa_own[d - 1, r, :, n * CHUNK:(n + 1) * CHUNK] = chunk_q(src, r, k, n)
            return carry

        lax.fori_loop(begin, begin + MOST, one, 0)

    def back(src, d, begin, low_row, high_row):
        def one(r, carry):
            _, filled = facts(src, r)
            acc[r // MOST] += filled * jnp.dot(sa_own[d - 1, r, :, low_row:high_row], d_w[src, r, low_row:high_row, :],
                                               preferred_element_type=F32)
            return carry

        lax.fori_loop(begin, begin + MOST, one, 0)

    whole(src_me, 0, 2 * MOST)
    for d in (1, 3, 2):
        src = source(d, False)
        remote(d_w.at[src], d_w.at[src], wz_s.at[d - 1], wz_r.at[d - 1], pair).wait_recv()
        whole(src, 0, 2 * MOST)
    for d in OFFSETS:
        a_out(d).wait_send()
    for d in OFFSETS:
        at = d_a.at[source(d, True), :, 0:UPPER, :]
        remote(at, at, apz_s.at[d - 1], apz_r.at[d - 1], pair).wait_recv()

    home = remote(acc.at[1 - h], part, o_s.at[0], o_r.at[0], pair)
    last = half - rows
    for t in range(2):
        tau = 1 - h if t == 0 else h
        begin = tau * MOST

        def got_low(d):
            at = low_at(source(d, True), tau)
            remote(at, at, al_s.at[d, t], al_r.at[d, t], pair).wait_recv()

        def got_w(d, i):
            at = d_w.at[source(d, True), pl.ds(begin, MOST), pl.ds(i * rows, rows), :]
            remote(at, at, wpz_s.at[i, d - 1, t], wpz_r.at[i, d - 1, t], pair).wait_recv()

        got_low(0)
        whole(src_pair, begin, MOST)
        for d in (1, 2, 3):
            got_low(d)
            front(source(d, True), d, begin)
        for d in OFFSETS:
            for i in range(PIECES - 1):
                got_w(d, i)
            back(source(d, True), d, begin, 0, last)
        for d in OFFSETS:
            got_w(d, PIECES - 1)
            back(source(d, True), d, begin, last, half)
        if t == 0:
            home.start()

    for j in range(1, 8):
        info_copy(j).wait_send()
    r_pair.wait_send()
    a_over.wait_send()
    for i in range(PIECES):
        w_over(i).wait_send()
    for d in OFFSETS:
        w_out(d).wait_send()
        ap_out(d).wait_send()
        for i in range(PIECES):
            for t in range(2):
                wp_out(i, d, t).wait_send()
    for d in range(4):
        for t in range(2):
            low(d, t).wait_send()
    for j in range(2):
        @pl.when(is_c)
        def _():
            op_c(j).wait_send()

        @pl.when(is_b)
        def _():
            op_b(j).wait_send()

        @pl.when(is_d)
        def _():
            op_d(j).wait_send()

        @pl.when(core == 0)
        def _():
            op_a(j).wait_send()
            op_e0(j).wait_send()

        @pl.when(core == 1)
        def _():
            op_e1(j).wait_send()

    home.wait()
    out_ref[...] = acc[h] + part[...]


def body(residual_traces, time_weights, lateral_amplitude, intersection_tile, visit_stop):
    traces, samples = residual_traces.shape
    blocks, _, depth = time_weights.shape
    lat = lateral_amplitude.shape[1]
    tiles = lax.axis_size("tile")
    half, slots = samples // 2, 2 * MOST
    rows = half // PIECES
    hops = tiles // 2 - 1
    dma = pltpu.SemaphoreType.DMA
    return pl.pallas_call(
        kernel,
        out_shape=jax.ShapeDtypeStruct((lat, depth), F32),
        in_specs=[pl.BlockSpec(memory_space=pl.ANY)] * 3 + [pl.BlockSpec(memory_space=pltpu.SMEM)] * 2,
        out_specs=pl.BlockSpec(memory_space=pltpu.VMEM),
        scratch_shapes=[
            pltpu.VMEM((2, STOPS, traces, half), BF16),
            pltpu.VMEM((blocks, lat, traces), BF16),
            pltpu.VMEM((blocks, half, depth), BF16),
            pltpu.VMEM((blocks, UPPER, traces), BF16),
            [pltpu.VMEM((blocks, rows, depth), BF16)] * PIECES,
            pltpu.VMEM((hops, slots, lat, traces), BF16),
            pltpu.VMEM((hops, slots, half, depth), BF16),
            pltpu.VMEM((hops, slots, UPPER, traces), BF16),
            pltpu.VMEM((PIECES, hops, slots, rows, depth), BF16),
            pltpu.VMEM((tiles, slots, lat, traces), BF16),
            pltpu.VMEM((tiles, slots, half, depth), BF16),
            pltpu.VMEM((tiles, 8, 128), jnp.int32),
            pltpu.SMEM((tiles, 8, 128), jnp.int32),
            pltpu.VMEM((2, lat, depth), F32),
            pltpu.VMEM((lat, depth), F32),
            dma((4,)), dma((8,)), dma((8,)), dma((6, 2)), dma((2, STOPS)),
            dma((hops,)), dma((hops,)), dma((hops,)), dma((hops,)), dma((1,)), dma((1,)),
            dma((PIECES,)), dma((PIECES,)), dma((hops,)), dma((hops,)), dma((PIECES, hops, 2)), dma((PIECES, hops, 2)),
            dma((4, 2)), dma((4, 2)), dma((1,)), dma((1,)),
        ],
        compiler_params=pltpu.CompilerParams(collective_id=0, has_side_effects=True, vmem_limit_bytes=60 << 20),
        cost_estimate=pl.CostEstimate(flops=10 << 30, bytes_accessed=12 << 20, transcendentals=0),
    )(residual_traces, time_weights, lateral_amplitude, intersection_tile.reshape(blocks), visit_stop)


def solution(mesh):
    assert mesh.shape["blk"] == 16 and mesh.shape["tile"] == 8
    in_specs = (
        P(("blk", "tile"), None),
        P(("blk", "tile"), None, None),
        P(("blk", "tile"), None, None),
        P(("blk", "tile"), None),
        P(("blk", "tile")),
    )
    out_specs = P(("blk", "tile"), None)
    return jax.shard_map(body, mesh=mesh, in_specs=in_specs, out_specs=out_specs, check_vma=False)
```

time: 177 us -> 172 us (0.972)
  Pallas kernels: 172 us -> 168 us
    pallas_call x1, Pallas kernels: 172 us -> 168 us  [body(): pl.pallas_call(kernel, out_shape=jax.ShapeDtypeStruct((lat, depth), F32),...]
where the time goes in v2:
time: 172 us; the launch traced here: 169 us
  Pallas kernels  168 us (98%)
    pallas_call x1, Pallas kernels, body(): pl.pallas_call(kernel, out_shape=jax.ShapeDtypeStruct((lat, depth), F32),...  168 us

profile of v2, /device:TPU:80, one launch (start us, length us, event | category | flops | bytes accessed | tf_op | source)
XLA Modules:
  0.0 169.4 jit_solution(2346802390746988194)
XLA Ops:
  0.0 168.0 %shard_map.55 = f32[128,128]{1,0:T(8,128)} custom-call(bf16[1024,2048]{1,0:T(8,128)(2,1)} %r_hbm.1, bf16[8,2048,128]{2,1,0:T(8,128)(2,1)} %w_hbm.1, bf16[8,128,1024]{2,1,0:T(8,128)(2,1)} %a_hbm.1, s32[8]{0:T(128)} %bitcast.1, s32[8]{0:T(128)} %stop_ref.1), custom_call_target="tpu_custom_call" | custom-call | flops 10737418240 | bytes 12582912 | tf_op jit(solution)/shard_map/pallas_call | solution.py:452
  168.0 1.5 copy.7

commit v3 on v2

--- a/solution.py
+++ b/solution.py
@@ -16,8 +16,8 @@
 BF16 = jnp.bfloat16
 
 
-def kernel(r_hbm, w_hbm, a_hbm, tile_ref, stop_ref, out_ref, r_all, a_own, w_own, a_pair, w_pair, sa_own, sw_own, sa_pair,
-           sw_pair, d_a, d_w, d_info, s_all, acc, part, loc, info_s, info_r, r_s, r_r, az_s, az_r, wz_s, wz_r,
+def kernel(r_hbm, w_hbm, a_hbm, tile_hbm, stop_hbm, out_ref, r_all, a_own, w_own, a_pair, w_pair, sa_own, sw_own, sa_pair,
+           sw_pair, d_a, d_w, d_info, tile_ref, stop_ref, s_all, acc, part, loc, info_s, info_r, r_s, r_r, az_s, az_r, wz_s, wz_r,
            ap_s, ap_r, wp_s, wp_r, apz_s, apz_r, wpz_s, wpz_r, al_s, al_r, o_s, o_r):
     blk, tile = lax.axis_index("blk"), lax.axis_index("tile")
     groups, tiles = lax.axis_size("blk"), lax.axis_size("tile")
@@ -50,6 +50,10 @@
     cp_a = pltpu.make_async_copy(a_hbm, a_own, loc.at[0])
     cp_r = pltpu.make_async_copy(r_hbm.at[:, mine], r_all.at[h, 0], loc.at[1])
     cp_w = pltpu.make_async_copy(w_hbm.at[:, mine, :], w_own, loc.at[2])
+    cp_tile = pltpu.make_async_copy(tile_hbm, tile_ref, loc.at[4])
+    cp_stop = pltpu.make_async_copy(stop_hbm, stop_ref, loc.at[5])
+    cp_tile.start()
+    cp_stop.start()
     cp_a.start()
     cp_r.start()
     cp_w.start()
@@ -79,6 +83,8 @@
     lane = lax.broadcasted_iota(jnp.int32, d_info.shape[1:], 1)
     line = lax.broadcasted_iota(jnp.int32, d_info.shape[1:], 0)
     info = jnp.zeros(d_info.shape[1:], jnp.int32)
+    cp_tile.wait()
+    cp_stop.wait()
     targets = [tile_ref[b] for b in range(blocks)]
     slot_of = []
     for b in range(blocks):
@@ -389,7 +395,6 @@
         for d in (1, 2, 3):
             got_low(d)
             front(source(d, True), d, begin)
-        for d in OFFSETS:
             for i in range(PIECES - 1):
                 got_w(d, i)
             back(source(d, True), d, begin, 0, last)
@@ -398,44 +403,47 @@
             back(source(d, True), d, begin, last, half)
         if t == 0:
             home.start()
-
-    for j in range(1, 8):
-        info_copy(j).wait_send()
-    r_pair.wait_send()
-    a_over.wait_send()
-    for i in range(PIECES):
-        w_over(i).wait_send()
-    for d in OFFSETS:
-        w_out(d).wait_send()
-        ap_out(d).wait_send()
+            for j in range(1, 8):
+                info_copy(j).wait_send()
+            r_pair.wait_send()
+            a_over.wait_send()
+            for i in range(PIECES):
+                w_over(i).wait_send()
+            for d in OFFSETS:
+                w_out(d).wait_send()
+                ap_out(d).wait_send()
+                for i in range(PIECES):
+                    wp_out(i, d, 0).wait_send()
+            for d in range(4):
+                low(d, 0).wait_send()
+            for j in range(2):
+                @pl.when(is_c)
+                def _():
+                    op_c(j).wait_send()
+
+                @pl.when(is_b)
+                def _():
+                    op_b(j).wait_send()
+
+                @pl.when(is_d)
+                def _():
+                    op_d(j).wait_send()
+
+                @pl.when(core == 0)
+                def _():
+                    op_a(j).wait_send()
+                    op_e0(j).wait_send()
+
+                @pl.when(core == 1)
+                def _():
+                    op_e1(j).wait_send()
+
+
+    for d in OFFSETS:
         for i in range(PIECES):
-            for t in range(2):
-                wp_out(i, d, t).wait_send()
+            wp_out(i, d, 1).wait_send()
     for d in range(4):
-        for t in range(2):
-            low(d, t).wait_send()
-    for j in range(2):
-        @pl.when(is_c)
-        def _():
-            op_c(j).wait_send()
-
-        @pl.when(is_b)
-        def _():
-            op_b(j).wait_send()
-
-        @pl.when(is_d)
-        def _():
-            op_d(j).wait_send()
-
-        @pl.when(core == 0)
-        def _():
-            op_a(j).wait_send()
-            op_e0(j).wait_send()
-
-        @pl.when(core == 1)
-        def _():
-            op_e1(j).wait_send()
-
+        low(d, 1).wait_send()
     home.wait()
     out_ref[...] = acc[h] + part[...]
 
@@ -452,7 +460,7 @@
     return pl.pallas_call(
         kernel,
         out_shape=jax.ShapeDtypeStruct((lat, depth), F32),
-        in_specs=[pl.BlockSpec(memory_space=pl.ANY)] * 3 + [pl.BlockSpec(memory_space=pltpu.SMEM)] * 2,
+        in_specs=[pl.BlockSpec(memory_space=pl.ANY)] * 5,
         out_specs=pl.BlockSpec(memory_space=pltpu.VMEM),
         scratch_shapes=[
             pltpu.VMEM((2, STOPS, traces, half), BF16),
@@ -467,10 +475,12 @@
             pltpu.VMEM((tiles, slots, lat, traces), BF16),
             pltpu.VMEM((tiles, slots, half, depth), BF16),
             pltpu.VMEM((tiles, 8, 128), jnp.int32),
+            pltpu.SMEM((blocks,), jnp.int32),
+            pltpu.SMEM((blocks,), jnp.int32),
             pltpu.SMEM((tiles, 8, 128), jnp.int32),
             pltpu.VMEM((2, lat, depth), F32),
             pltpu.VMEM((lat, depth), F32),
-            dma((4,)), dma((8,)), dma((8,)), dma((6, 2)), dma((2, STOPS)),
+            dma((6,)), dma((8,)), dma((8,)), dma((6, 2)), dma((2, STOPS)),
             dma((hops,)), dma((hops,)), dma((hops,)), dma((hops,)), dma((1,)), dma((1,)),
             dma((PIECES,)), dma((PIECES,)), dma((hops,)), dma((hops,)), dma((PIECES, hops, 2)), dma((PIECES, hops, 2)),
             dma((4, 2)), dma((4, 2)), dma((1,)), dma((1,)),

time: 172 us -> 170 us (0.988)
  Pallas kernels: 168 us -> 166 us
where the time goes in v3:
time: 170 us; the launch traced here: 168 us
  Pallas kernels  166 us (98%)
    pallas_call x1, Pallas kernels, body(): pl.pallas_call(kernel, out_shape=jax.ShapeDtypeStruct((lat, depth), F32),...  166 us

profile of v3, /device:TPU:80, one launch (start us, length us, event | category | flops | bytes accessed | tf_op | source)
XLA Modules:
  0.0 167.9 jit_solution(16194514974985739937)
XLA Ops:
  0.0 166.4 %shard_map.55 = f32[128,128]{1,0:T(8,128)} custom-call(bf16[1024,2048]{1,0:T(8,128)(2,1)} %r_hbm.1, bf16[8,2048,128]{2,1,0:T(8,128)(2,1)} %w_hbm.1, bf16[8,128,1024]{2,1,0:T(8,128)(2,1)} %a_hbm.1, s32[8]{0:T(128)} %bitcast.1, s32[8]{0:T(128)} %stop_hbm.1), custom_call_target="tpu_custom_call" | custom-call | flops 10737418240 | bytes 12582912 | tf_op jit(solution)/shard_map/pallas_call | solution.py:460
  166.4 1.5 copy.7

commit v4 on v3

--- a/solution.py
+++ b/solution.py
@@ -47,6 +47,28 @@
     def lane_of(d):
         return (blk, ((z + d) % zs) * 2 + h)
 
+    barrier = pltpu.get_barrier_semaphore()
+
+    def greet(where):
+        pl.semaphore_signal(barrier, inc=1, device_id=where, device_id_type=MESH)
+
+    for j in range(1, 8):
+        greet((blk, (tile + j) % tiles))
+    greet(sibling)
+    from_yh0_odd = (yh == 0) & (core == 1)
+
+    @pl.when(from_yh0_odd)
+    def _():
+        greet(((blk + 1) % groups, z * 2 + 1 - h))
+
+    @pl.when(jnp.logical_not(from_yh0_odd))
+    def _():
+        greet(((blk + groups - 2) % groups, z * 2 + 1 - h))
+
+    @pl.when(core == 0)
+    def _():
+        greet(((blk + groups - 3) % groups, tile))
+
     cp_a = pltpu.make_async_copy(a_hbm, a_own, loc.at[0])
     cp_r = pltpu.make_async_copy(r_hbm.at[:, mine], r_all.at[h, 0], loc.at[1])
     cp_w = pltpu.make_async_copy(w_hbm.at[:, mine, :], w_own, loc.at[2])
@@ -57,28 +79,6 @@
     cp_a.start()
     cp_r.start()
     cp_w.start()
-
-    barrier = pltpu.get_barrier_semaphore()
-
-    def greet(where):
-        pl.semaphore_signal(barrier, inc=1, device_id=where, device_id_type=MESH)
-
-    for j in range(1, 8):
-        greet((blk, (tile + j) % tiles))
-    greet(sibling)
-    from_yh0_odd = (yh == 0) & (core == 1)
-
-    @pl.when(from_yh0_odd)
-    def _():
-        greet(((blk + 1) % groups, z * 2 + 1 - h))
-
-    @pl.when(jnp.logical_not(from_yh0_odd))
-    def _():
-        greet(((blk + groups - 2) % groups, z * 2 + 1 - h))
-
-    @pl.when(core == 0)
-    def _():
-        greet(((blk + groups - 3) % groups, tile))
 
     lane = lax.broadcasted_iota(jnp.int32, d_info.shape[1:], 1)
     line = lax.broadcasted_iota(jnp.int32, d_info.shape[1:], 0)
@@ -220,12 +220,16 @@
     def source(d, flip):
         return ((z + zs - d) % zs) * 2 + (1 - h if flip else h)
 
-    def low_at(src, tau):
-        return d_a.at[src, pl.ds(tau * MOST, MOST), UPPER:lat, :]
-
-    def low(d, t):
-        at = low_at(source(d, False), h if t == 0 else 1 - h)
-        return remote(at, at, al_s.at[d, t], al_r.at[d, t], pair)
+    lows = [(d, t, 0, MOST) for t in range(2) for d in range(4)]
+    lows[-1:] = [(3, 1, i, 1) for i in range(MOST)]
+
+    def low_at(src, tau, skip, count):
+        return d_a.at[src, pl.ds(tau * MOST + skip, count), UPPER:lat, :]
+
+    def low(n):
+        d, t, skip, count = lows[n]
+        at = low_at(source(d, False), h if t == 0 else 1 - h, skip, count)
+        return remote(at, at, al_s.at[n], al_r.at[n], pair)
 
     cp_w.wait()
     for d in OFFSETS:
@@ -291,28 +295,22 @@
 
     for d in (1, 3, 2):
         got_own_a(d)
-    for t in range(2):
-        for d in range(4):
-            low(d, t).start()
+    for n in range(len(lows)):
+        low(n).start()
 
     @pl.when(core == 0)
     def _():
         arrive_3(0)
 
     forward(1)
-    w_over(0).wait_recv()
-    relay_piece(0, 0)
-    w_over(1).wait_recv()
-    relay_piece(1, 0)
-
-    @pl.when(core == 0)
-    def _():
-        arrive_3(1)
-
-    w_over(2).wait_recv()
-    relay_piece(2, 0)
-    w_over(3).wait_recv()
-    relay_piece(3, 0)
+    for i in range(PIECES):
+        w_over(i).wait_recv()
+        relay_piece(i, 0)
+        if i == PIECES // 2 - 1:
+            @pl.when(core == 0)
+            def _():
+                arrive_3(1)
+
     for i in range(PIECES):
         relay_piece(i, 1)
     forward(0)
@@ -347,14 +345,14 @@
 
         lax.fori_loop(begin, begin + count, one, 0)
 
-    def front(src, d, begin):
+    def front(src, d, begin, count):
         def one(r, carry):
             k, _ = facts(src, r)
             for n in range(half // CHUNK):
                 sa_own[d - 1, r, :, n * CHUNK:(n + 1) * CHUNK] = chunk_q(src, r, k, n)
             return carry
 
-        lax.fori_loop(begin, begin + MOST, one, 0)
+        lax.fori_loop(begin, begin + count, one, 0)
 
     def back(src, d, begin, low_row, high_row):
         def one(r, carry):
@@ -382,19 +380,22 @@
         tau = 1 - h if t == 0 else h
         begin = tau * MOST
 
-        def got_low(d):
-            at = low_at(source(d, True), tau)
-            remote(at, at, al_s.at[d, t], al_r.at[d, t], pair).wait_recv()
+        def got_low(n):
+            d, _, skip, count = lows[n]
+            at = low_at(source(d, True), tau, skip, count)
+            remote(at, at, al_s.at[n], al_r.at[n], pair).wait_recv()
 
         def got_w(d, i):
             at = d_w.at[source(d, True), pl.ds(begin, MOST), pl.ds(i * rows, rows), :]
             remote(at, at, wpz_s.at[i, d - 1, t], wpz_r.at[i, d - 1, t], pair).wait_recv()
 
-        got_low(0)
+        got_low(4 * t)
         whole(src_pair, begin, MOST)
         for d in (1, 2, 3):
-            got_low(d)
-            front(source(d, True), d, begin)
+            for n in range(4 * t, len(lows)):
+                if lows[n][:2] == (d, t):
+                    got_low(n)
+                    front(source(d, True), d, begin + lows[n][2], lows[n][3])
             for i in range(PIECES - 1):
                 got_w(d, i)
             back(source(d, True), d, begin, 0, last)
@@ -415,7 +416,7 @@
                 for i in range(PIECES):
                     wp_out(i, d, 0).wait_send()
             for d in range(4):
-                low(d, 0).wait_send()
+                low(d).wait_send()
             for j in range(2):
                 @pl.when(is_c)
                 def _():
@@ -442,8 +443,8 @@
     for d in OFFSETS:
         for i in range(PIECES):
             wp_out(i, d, 1).wait_send()
-    for d in range(4):
-        low(d, 1).wait_send()
+    for n in range(4, len(lows)):
+        low(n).wait_send()
     home.wait()
     out_ref[...] = acc[h] + part[...]
 
@@ -483,7 +484,7 @@
             dma((6,)), dma((8,)), dma((8,)), dma((6, 2)), dma((2, STOPS)),
             dma((hops,)), dma((hops,)), dma((hops,)), dma((hops,)), dma((1,)), dma((1,)),
             dma((PIECES,)), dma((PIECES,)), dma((hops,)), dma((hops,)), dma((PIECES, hops, 2)), dma((PIECES, hops, 2)),
-            dma((4, 2)), dma((4, 2)), dma((1,)), dma((1,)),
+            dma((9,)), dma((9,)), dma((1,)), dma((1,)),
         ],
         compiler_params=pltpu.CompilerParams(collective_id=0, has_side_effects=True, vmem_limit_bytes=60 << 20),
         cost_estimate=pl.CostEstimate(flops=10 << 30, bytes_accessed=12 << 20, transcendentals=0),

time: 170 us -> 170 us (level)
  no operation moved by 1% of the time
where the time goes in v4:
time: 170 us; the launch traced here: 167 us
  Pallas kernels  166 us (98%)
    pallas_call x1, Pallas kernels, body(): pl.pallas_call(kernel, out_shape=jax.ShapeDtypeStruct((lat, depth), F32),...  166 us

profile of v4, /device:TPU:80, one launch (start us, length us, event | category | flops | bytes accessed | tf_op | source)
XLA Modules:
  0.0 167.4 jit_solution(5065616453562115824)
XLA Ops:
  0.0 166.0 %shard_map.55 = f32[128,128]{1,0:T(8,128)} custom-call(bf16[1024,2048]{1,0:T(8,128)(2,1)} %r_hbm.1, bf16[8,2048,128]{2,1,0:T(8,128)(2,1)} %w_hbm.1, bf16[8,128,1024]{2,1,0:T(8,128)(2,1)} %a_hbm.1, s32[8]{0:T(128)} %bitcast.1, s32[8]{0:T(128)} %stop_hbm.1), custom_call_target="tpu_custom_call" | custom-call | flops 10737418240 | bytes 12582912 | tf_op jit(solution)/shard_map/pallas_call | solution.py:461
  166.0 1.5 copy.7
